TPU v7x, 256 devices: a whole 4x4x8 slice. The times are simulated.
256 devices in a mesh: row: 8 (over z), col: 32 (over x, y, core).
Axes of the slice: x: 4, y: 4, z: 8, core: 2. Of those that a mesh axis runs over, the one named last changes fastest.
Arguments:
- embeddings: bfloat16 [49152, 256], P(('row', 'col')), may hold values from -256 to 256
- start_vectors: float32 [49152, 64], P(('row', 'col')), may hold values from -6 to 6
Outputs:
- spectral: float32 [49152, 64], P(('row', 'col'))
All inputs are finite; a program needn't handle non-finite values.
Results may differ from a plain program's by a relative error of at most 0.0068.
Values may be sent and summed in bfloat16 or wider, within the bound.
No kernel may reach another device: no remote copies, remote signals or barrier semaphores. Data moves between devices by JAX's collectives and lax.ppermute only.
A program may use at most 64 MiB of HBM per device.

v0:
```python
import math
import jax
import jax.numpy as jnp
from jax import lax
from jax.sharding import PartitionSpec as P

sharpness = 16.0
threshold = 0.3


def local(embeddings, start_vectors):
    local_docs = embeddings.shape[0]
    all_docs = local_docs * lax.axis_size("row") * lax.axis_size("col")
    widened = embeddings.astype(jnp.float32)
    unit_rows = (
        widened * lax.rsqrt(jnp.sum(widened * widened, axis=1, keepdims=True) + 1e-06)
    ).astype(jnp.bfloat16)
    column_set = lax.all_gather(unit_rows, "row", axis=0, tiled=True)
    scores = lax.dot_general(
        lax.all_gather(unit_rows, "col", axis=0, tiled=True),
        column_set,
        (((1,), (1,)), ((), ())),
        preferred_element_type=jnp.float32,
    )
    adjacency = jax.nn.sigmoid(sharpness * (scores - threshold)).astype(jnp.bfloat16)
    row_sums = jnp.sum(adjacency, axis=1, dtype=jnp.float32)
    degree_set = lax.psum(row_sums, "col")
    own_first = lax.axis_index("col") * local_docs
    degree = lax.dynamic_slice_in_dim(degree_set, own_first, local_docs, 0)
    inv_root = lax.rsqrt(degree)
    root_degree = jnp.sqrt(degree)

    def products(weighted):
        gathered = lax.all_gather(weighted, "row", axis=0, tiled=True)
        return (adjacency, gathered)

    def own_sums(weighted):
        tiles, gathered = products(weighted)
        return lax.psum_scatter(
            jnp.dot(tiles, gathered, preferred_element_type=jnp.float32),
            "col",
            scatter_dimension=0,
            tiled=True,
        )

    def deflation(vectors):
        return lax.psum(
            (jnp.sum(root_degree[:, None] * vectors, axis=0), jnp.sum(degree)), ("row", "col")
        )

    vectors = start_vectors
    weighted = (inv_root[:, None] * vectors).astype(jnp.bfloat16)
    correlation, degree_total = deflation(vectors)
    partial_sums = own_sums(weighted)
    vectors = (
        inv_root[:, None] * partial_sums
        - root_degree[:, None] * (correlation / degree_total)[None, :]
    )
    weighted = (inv_root[:, None] * vectors).astype(jnp.bfloat16)
    correlation, degree_total = deflation(vectors)
    partial_sums = own_sums(weighted)
    vectors = (
        inv_root[:, None] * partial_sums
        - root_degree[:, None] * (correlation / degree_total)[None, :]
    )
    gram_matrix = lax.psum(
        jnp.dot(vectors.T, vectors, precision=lax.Precision.HIGHEST), ("row", "col")
    )
    cholesky_factor = jnp.linalg.cholesky(gram_matrix)
    solved = lax.linalg.triangular_solve(cholesky_factor, vectors.T, left_side=True, lower=True)
    return solved.T * math.sqrt(all_docs)


def solution(mesh):
    return jax.shard_map(
        local,
        mesh=mesh,
        in_specs=(P(("row", "col"), None), P(("row", "col"), None)),
        out_specs=P(("row", "col"), None),
        check_vma=False,
    )
```

profile of v0, /device:TPU:1, one launch (start us, length us, event | category | flops | bytes accessed | tf_op | source)
XLA Modules:
  0.0 554.0 jit_solution(9075832216609413625)
XLA Ops:
  6.5 1.0 fusion
  7.6 1.6 fusion.1
  9.2 24.6 %all_gather.13 = bf16[1536,256]{1,0:T(8,128)(2,1)S(1)} all-gather(bf16[192,256]{1,0:T(8,128)(2,1)} %fusion.1), channel_id=1, replica_groups=mesh['row'=8,'col'=32] {'row'}, dimensions={0}, use_global_device_ids=true | all-gather | bytes 884736 | tf_op jit(solution)/shard_map/all_gather | solution.py:18
  33.9 30.4 %all-gather.4.cloned.1.call-done = bf16[6144,256]{1,0:T(8,128)(2,1)} async-done(((bf16[192,256]{1,0:T(8,128)(2,1)}), bf16[6144,256]{1,0:T(8,128)(2,1)}) %all-gather.4.cloned.1.call-update) | async-done | bytes 3145744 | tf_op jit(solution)/shard_map/all_gather | solution.py:20
  64.2 16.3 %convert_reduce_fusion = (f32[6144]{0:T(1024)S(1)}, bf16[6144,1536]{0,1:T(8,128)(2,1)}) fusion(bf16[6144,256]{1,0:T(8,128)(2,1)} %all-gather.4.cloned.1.call-done, bf16[1536,256]{1,0:T(8,128)(2,1)S(1)} %all_gather.13), kind=kOutput, calls=%fused_computation | convolution fusion | flops 4907329536 | bytes 22831104 | tf_op jit(solution)/shard_map/dot_general | solution.py:19
  80.5 120.9 %psum.38 = f32[6144]{0:T(1024)S(1)} all-reduce(f32[6144]{0:T(1024)S(1)} %get-tuple-element.14), channel_id=1, replica_groups=mesh['row'=8,'col'=32] {'col'}, use_global_device_ids=true, to_apply=%region_2.0 | all-reduce | flops 6144 | bytes 49152 | tf_op jit(solution)/shard_map/psum | solution.py:27
  201.4 0.7 dynamic-slice_reduce_fusion
  202.1 0.1 multiply_reduce_fusion.1
  202.2 19.9 %all-gather = bf16[8,192,64]{1,2,0:T(8,128)(2,1)S(1)} all-gather(bf16[1,192,64]{1,2,0:T(8,128)(2,1)S(1)} %get-tuple-element.10), channel_id=1, replica_groups=mesh['row'=8,'col'=32] {'row'}, dimensions={0}, use_global_device_ids=true | all-gather | bytes 221184 | tf_op jit(solution)/shard_map/all_gather | solution.py:34
  222.1 0.1 copy.9
  222.2 0.2 reshape.20
  222.4 12.9 %fusion.14 = f32[6144,64]{1,0:T(8,128)} fusion(bf16[1536,64]{0,1:T(8,128)(2,1)S(1)} %reshape.20, bf16[6144,1536]{0,1:T(8,128)(2,1)} %get-tuple-element.15), kind=kOutput, calls=%fused_computation.37 | convolution fusion | flops 1207959552 | bytes 20643840
  235.5 83.2 %all-reduce = (f32[64]{0:T(128)S(1)}, f32[]{:T(128)}) all-reduce(f32[64]{0:T(128)S(1)} %get-tuple-element.9, f32[]{:T(128)} %get-tuple-element.11), channel_id=1, replica_groups=mesh['row'=8,'col'=32] {'row','col'}, use_global_device_ids=true, to_apply=%region_5.0 | all-reduce | flops 65 | bytes 520 | tf_op jit(solution)/shard_map/psum | solution.py:47
  318.7 0.6 broadcast_divide_fusion.1
  319.3 9.1 %reduce-scatter.7.cloned.1.call-done = f32[192,64]{1,0:T(8,128)} async-done(((f32[6144,64]{1,0:T(8,128)}), f32[192,64]{1,0:T(8,128)}) %reduce-scatter.7.cloned.1.call-update) | async-done | bytes 49168
  328.4 1.0 copy.15
  329.4 0.2 multiply_reduce_fusion
  329.5 20.3 %all-gather.1 = bf16[8,192,64]{1,2,0:T(8,128)(2,1)S(1)} all-gather(bf16[1,192,64]{1,2,0:T(8,128)(2,1)S(1)} %get-tuple-element.8), channel_id=1, replica_groups=mesh['row'=8,'col'=32] {'row'}, dimensions={0}, use_global_device_ids=true | all-gather | bytes 221184 | tf_op jit(solution)/shard_map/all_gather | solution.py:34
  349.8 0.1 copy.10
  350.0 0.2 reshape.22
  350.2 12.9 %fusion.15 = f32[6144,64]{1,0:T(8,128)} fusion(bf16[1536,64]{0,1:T(8,128)(2,1)S(1)} %reshape.22, bf16[6144,1536]{0,1:T(8,128)(2,1)} %get-tuple-element.15), kind=kOutput, calls=%fused_computation.38 | convolution fusion | flops 1207959552 | bytes 20643840
  363.2 81.8 %psum.41 = f32[64]{0:T(128)S(1)} all-reduce(f32[64]{0:T(128)S(1)} %get-tuple-element.7), channel_id=1, replica_groups=mesh['row'=8,'col'=32] {'row','col'}, use_global_device_ids=true, to_apply=%region_10.0 | all-reduce | flops 64 | bytes 512 | tf_op jit(solution)/shard_map/psum | solution.py:47
  445.0 0.6 broadcast_divide_fusion
  445.7 10.1 %reduce-scatter.9.cloned.1.call-done = f32[192,64]{1,0:T(8,128)} async-done(((f32[6144,64]{1,0:T(8,128)}), f32[192,64]{1,0:T(8,128)}) %reduce-scatter.9.cloned.1.call-update) | async-done | bytes 49168
  455.8 1.0 copy.17
  456.8 0.3 fusion.2
  457.0 77.3 %psum.42 = f32[64,64]{0,1:T(8,128)S(1)} all-reduce(f32[64,64]{0,1:T(8,128)S(1)} %fusion.2), channel_id=1, replica_groups=mesh['row'=8,'col'=32] {'row','col'}, use_global_device_ids=true, to_apply=%region_11.0 | all-reduce | flops 4096 | bytes 32768 | tf_op jit(solution)/shard_map/psum | solution.py:66
  534.4 5.8 %cholesky.16 = f32[64,64]{1,0:T(8,128)S(1)} custom-call(f32[64,64]{1,0:T(8,128)S(1)} %fusion.7), custom_call_target="Cholesky" | custom-call | tf_op jit(solution)/shard_map/jit(cholesky)/cholesky | solution.py:69
  540.3 0.6 compare_reduce_fusion
  540.9 0.7 fusion.3
  541.6 4.9 custom-call.6
  546.5 0.9 convolution_multiply_fusion
  (12 shorter events, 0.3 us)
Async XLA Ops:
  6.5 57.7 %all-gather.4.cloned.1.call-start = ((), (), s32[]{:S(2)}) async-start(), calls=%async_computation.2 | async-start | bytes 3244032 | tf_op jit(solution)/shard_map/all_gather | solution.py:20
  9.2 319.2 %reduce-scatter.7.cloned.1.call-start = ((), (), s32[]{:S(2)}) async-start(), calls=%async_computation.3 | async-start | bytes 3244032
  33.9 168.2 %copy-start = (f32[192,64]{0,1:T(8,128)S(1)}, f32[192,64]{0,1:T(8,128)}, u32[]{:S(2)}) copy-start(f32[192,64]{0,1:T(8,128)} %param.3) | copy-start | bytes 147460
  235.4 220.4 %reduce-scatter.9.cloned.1.call-start = ((), (), s32[]{:S(2)}) async-start(), calls=%async_computation.4 | async-start | bytes 3244032
Sparse Core Ops, SparseCore 0:
  9.9 54.2 all-gather.3
  235.5 92.8 reduce-scatter.6
  363.3 92.4 reduce-scatter.8
where the time goes:
time: 555 us; the launch traced here: 554 us
  blocking collectives  428 us (77%)
  waiting for transfers between devices  49.6 us (9%)
  matrix products  43.3 us (8%)
  other arithmetic  17 us (3%)
  between operations  13.2 us (2%)
    psum x2, blocking collectives, deflation(): lax.psum((jnp.sum(root_degree[:, None] * vectors, axis=0), jnp.sum(degree...  165 us
    psum x1, blocking collectives, local(): degree_set = lax.psum(row_sums, 'col')  121 us
    psum x1, blocking collectives, local(): lax.psum(jnp.dot(vectors.T, vectors, precision=lax.Precision.HIGHEST), ('...  77.3 us
    all_gather x2, blocking collectives, products(): gathered = lax.all_gather(weighted, 'row', axis=0, tiled=True)  40.2 us
    all_gather x1, waiting for transfers between devices, local(): lax.all_gather(unit_rows, 'col', axis=0, tiled=True)  30.4 us
    unnamed x2, matrix products  25.9 us
    all_gather x1, blocking collectives, local(): column_set = lax.all_gather(unit_rows, 'row', axis=0, tiled=True)  24.6 us
    unnamed x5, waiting for transfers between devices  19.2 us
  transfers between devices with their start and end apart: 3, of which 3 were waited for; matrix products, arithmetic and copies ran while one was open for 0% of the time, Pallas kernels for 0%

commit v1 on v0

--- a/solution.py
+++ b/solution.py
@@ -6,6 +6,12 @@
 
 sharpness = 16.0
 threshold = 0.3
+
+
+def add_all(value, mesh_axis):
+    parts = lax.all_gather(value, mesh_axis, axis=0, tiled=False)
+    total = parts.sum(axis=0)
+    return total
 
 
 def local(embeddings, start_vectors):
@@ -63,7 +69,7 @@
         inv_root[:, None] * partial_sums
         - root_degree[:, None] * (correlation / degree_total)[None, :]
     )
-    gram_matrix = lax.psum(
+    gram_matrix = add_all(
         jnp.dot(vectors.T, vectors, precision=lax.Precision.HIGHEST), ("row", "col")
     )
     cholesky_factor = jnp.linalg.cholesky(gram_matrix)

time: 555 us -> 603 us (1.086)
  waiting for transfers between devices: 49.6 us -> 171 us
  blocking collectives: 428 us -> 351 us
    all_gather x0 -> x1, waiting for transfers between devices: none -> 121 us  [add_all(): parts = lax.all_gather(value, mesh_axis, axis=0, tiled=False)]
    psum x1 -> x0, blocking collectives: 77.3 us -> none  [local(): lax.psum(jnp.dot(vectors.T, vectors, precision=lax.Precision.HIGHEST), ('...]
    unnamed x5 -> x6, waiting for transfers between devices: 19.2 us -> 19.2 us
  transfers between devices with their start and end apart: 3 -> 4, of which waited for: 3 -> 4; matrix products, arithmetic and copies ran while one was open for 0% -> 0% of each run, Pallas kernels for 0% -> 0%
where the time goes in v1:
time: 603 us
  blocking collectives  351 us (58%)
  waiting for transfers between devices  171 us (28%)
  matrix products  44 us (7%)
  other arithmetic  21 us (3%)
  between operations  13.2 us (2%)
    psum x2, blocking collectives, deflation(): lax.psum((jnp.sum(root_degree[:, None] * vectors, axis=0), jnp.sum(degree...  165 us
    all_gather x1, waiting for transfers between devices, add_all(): parts = lax.all_gather(value, mesh_axis, axis=0, tiled=False)  121 us
    psum x1, blocking collectives, local(): degree_set = lax.psum(row_sums, 'col')  121 us
    all_gather x2, blocking collectives, products(): gathered = lax.all_gather(weighted, 'row', axis=0, tiled=True)  40.2 us
    all_gather x1, waiting for transfers between devices, local(): lax.all_gather(unit_rows, 'col', axis=0, tiled=True)  30.4 us
    unnamed x2, matrix products  25.9 us
    all_gather x1, blocking collectives, local(): column_set = lax.all_gather(unit_rows, 'row', axis=0, tiled=True)  24.6 us
    unnamed x6, waiting for transfers between devices  19.2 us
  transfers between devices with their start and end apart: 4, of which 4 were waited for; matrix products, arithmetic and copies ran while one was open for 0% of the time, Pallas kernels for 0%

profile of v1, /device:TPU:1, one launch (start us, length us, event | category | flops | bytes accessed | tf_op | source)
XLA Modules:
  0.0 602.7 jit_solution(8586219813445780514)
XLA Ops:
  6.5 1.0 fusion
  7.6 1.6 fusion.1
  9.2 24.6 %all_gather.19 = bf16[1536,256]{1,0:T(8,128)(2,1)S(1)} all-gather(bf16[192,256]{1,0:T(8,128)(2,1)} %fusion.1), channel_id=1, replica_groups=mesh['row'=8,'col'=32] {'row'}, dimensions={0}, use_global_device_ids=true | all-gather | bytes 884736 | tf_op jit(solution)/shard_map/all_gather | solution.py:24
  33.9 30.4 %all-gather.6.cloned.1.call-done = bf16[6144,256]{1,0:T(8,128)(2,1)} async-done(((bf16[192,256]{1,0:T(8,128)(2,1)}), bf16[6144,256]{1,0:T(8,128)(2,1)}) %all-gather.6.cloned.1.call-update) | async-done | bytes 3145744 | tf_op jit(solution)/shard_map/all_gather | solution.py:26
  64.2 16.3 %convert_reduce_fusion = (f32[6144]{0:T(1024)S(1)}, bf16[6144,1536]{0,1:T(8,128)(2,1)}) fusion(bf16[6144,256]{1,0:T(8,128)(2,1)} %all-gather.6.cloned.1.call-done, bf16[1536,256]{1,0:T(8,128)(2,1)S(1)} %all_gather.19), kind=kOutput, calls=%fused_computation | convolution fusion | flops 4907329536 | bytes 22831104 | tf_op jit(solution)/shard_map/dot_general | solution.py:25
  80.5 120.9 %psum.31 = f32[6144]{0:T(1024)S(1)} all-reduce(f32[6144]{0:T(1024)S(1)} %get-tuple-element.14), channel_id=1, replica_groups=mesh['row'=8,'col'=32] {'col'}, use_global_device_ids=true, to_apply=%region_2.0 | all-reduce | flops 6144 | bytes 49152 | tf_op jit(solution)/shard_map/psum | solution.py:33
  201.4 0.7 dynamic-slice_reduce_fusion
  202.2 19.9 %all-gather.1 = bf16[8,192,64]{1,2,0:T(8,128)(2,1)S(1)} all-gather(bf16[1,192,64]{1,2,0:T(8,128)(2,1)S(1)} %get-tuple-element.10), channel_id=1, replica_groups=mesh['row'=8,'col'=32] {'row'}, dimensions={0}, use_global_device_ids=true | all-gather | bytes 221184 | tf_op jit(solution)/shard_map/all_gather | solution.py:40
  222.1 0.1 copy.7
  222.2 0.2 reshape.21
  222.5 12.9 %fusion.14 = f32[6144,64]{1,0:T(8,128)} fusion(bf16[1536,64]{0,1:T(8,128)(2,1)S(1)} %reshape.21, bf16[6144,1536]{0,1:T(8,128)(2,1)} %get-tuple-element.15), kind=kOutput, calls=%fused_computation.37 | convolution fusion | flops 1207959552 | bytes 20643840
  235.5 83.2 %all-reduce = (f32[64]{0:T(128)S(1)}, f32[]{:T(128)}) all-reduce(f32[64]{0:T(128)S(1)} %get-tuple-element.9, f32[]{:T(128)} %get-tuple-element.11), channel_id=1, replica_groups=mesh['row'=8,'col'=32] {'row','col'}, use_global_device_ids=true, to_apply=%region_5.0 | all-reduce | flops 65 | bytes 520 | tf_op jit(solution)/shard_map/psum | solution.py:53
  318.7 0.6 broadcast_divide_fusion.1
  319.3 9.1 %reduce-scatter.7.cloned.1.call-done = f32[192,64]{1,0:T(8,128)} async-done(((f32[6144,64]{1,0:T(8,128)}), f32[192,64]{1,0:T(8,128)}) %reduce-scatter.7.cloned.1.call-update) | async-done | bytes 49168
  328.4 1.0 copy.11
  329.4 0.2 multiply_reduce_fusion
  329.5 20.3 %all-gather.2 = bf16[8,192,64]{1,2,0:T(8,128)(2,1)S(1)} all-gather(bf16[1,192,64]{1,2,0:T(8,128)(2,1)S(1)} %get-tuple-element.8), channel_id=1, replica_groups=mesh['row'=8,'col'=32] {'row'}, dimensions={0}, use_global_device_ids=true | all-gather | bytes 221184 | tf_op jit(solution)/shard_map/all_gather | solution.py:40
  349.8 0.1 copy.8
  350.0 0.2 reshape.23
  350.2 12.9 %fusion.15 = f32[6144,64]{1,0:T(8,128)} fusion(bf16[1536,64]{0,1:T(8,128)(2,1)S(1)} %reshape.23, bf16[6144,1536]{0,1:T(8,128)(2,1)} %get-tuple-element.15), kind=kOutput, calls=%fused_computation.38 | convolution fusion | flops 1207959552 | bytes 20643840
  363.2 81.8 %psum.34 = f32[64]{0:T(128)S(1)} all-reduce(f32[64]{0:T(128)S(1)} %get-tuple-element.7), channel_id=1, replica_groups=mesh['row'=8,'col'=32] {'row','col'}, use_global_device_ids=true, to_apply=%region_10.0 | all-reduce | flops 64 | bytes 512 | tf_op jit(solution)/shard_map/psum | solution.py:53
  445.1 0.6 broadcast_divide_fusion
  445.7 10.1 %reduce-scatter.9.cloned.1.call-done = f32[192,64]{1,0:T(8,128)} async-done(((f32[6144,64]{1,0:T(8,128)}), f32[192,64]{1,0:T(8,128)}) %reduce-scatter.9.cloned.1.call-update) | async-done | bytes 49168
  455.8 1.0 copy.13
  456.8 0.9 fusion.2
  457.7 121.4 %all-gather.8.cloned.1.call-done = f32[16384,64]{1,0:T(8,128)} async-done(((f32[64,64]{1,0:T(8,128)}), f32[16384,64]{1,0:T(8,128)}) %all-gather.8.cloned.1.call-update) | async-done | bytes 4194320 | tf_op jit(solution)/shard_map/all_gather | solution.py:12
  579.1 4.0 reduce_sum.63
  583.2 5.8 cholesky.16
  589.1 0.6 compare_reduce_fusion
  589.7 0.7 fusion.3
  590.4 4.9 custom-call.6
  595.3 0.9 convolution_multiply_fusion
  (15 shorter events, 0.4 us)
Async XLA Ops:
  6.5 57.7 %all-gather.6.cloned.1.call-start = ((), (), s32[]{:S(2)}) async-start(), calls=%async_computation.2 | async-start | bytes 3244032 | tf_op jit(solution)/shard_map/all_gather | solution.py:26
  9.2 319.2 %reduce-scatter.7.cloned.1.call-start = ((), (), s32[]{:S(2)}) async-start(), calls=%async_computation.4 | async-start | bytes 3244032
  33.9 168.2 %copy-start = (f32[192,64]{0,1:T(8,128)S(1)}, f32[192,64]{0,1:T(8,128)}, u32[]{:S(2)}) copy-start(f32[192,64]{0,1:T(8,128)} %param.3) | copy-start | bytes 147460
  235.4 220.4 %reduce-scatter.9.cloned.1.call-start = ((), (), s32[]{:S(2)}) async-start(), calls=%async_computation.5 | async-start | bytes 3244032
  363.2 215.9 %all-gather.8.cloned.1.call-start = ((), (), s32[]{:S(2)}) async-start(), calls=%async_computation.3 | async-start | bytes 8421376 | tf_op jit(solution)/shard_map/all_gather | solution.py:12
Sparse Core Ops, SparseCore 0:
  9.9 54.2 all-gather.5
  235.5 92.8 reduce-scatter.6
  363.3 92.4 reduce-scatter.8
  459.4 119.6 all-gather.7

commit v2 on v0

--- a/solution.py
+++ b/solution.py
@@ -31,7 +31,15 @@
     root_degree = jnp.sqrt(degree)
 
     def products(weighted):
-        gathered = lax.all_gather(weighted, "row", axis=0, tiled=True)
+        axis_n = jax.lax.psum(1, axis_name="row")
+        by_rank = tuple(((jj, (jj + 1) % axis_n) for jj in range(axis_n)))
+        now = [None] * axis_n
+        now[axis_n - 1] = weighted
+        for kk in range(axis_n - 2, -1, -1):
+            now[kk] = jax.lax.ppermute(now[kk + 1], axis_name="row", perm=by_rank)
+        outer = jnp.concatenate(now, 0)
+        built = (jax.lax.axis_index("row") + 1) * weighted.shape[0]
+        gathered = jnp.roll(outer, built, 0)
         return (adjacency, gathered)
 
     def own_sums(weighted):

time: 555 us -> 577 us (1.040)
  waiting for transfers between devices: 49.6 us -> 106 us
  blocking collectives: 428 us -> 391 us
    ppermute x0 -> x14, waiting for transfers between devices: none -> 54.4 us  [products(): now[kk] = jax.lax.ppermute(now[kk + 1], axis_name='row', perm=by_rank)]
    all_gather x2 -> x0, blocking collectives: 40.2 us -> none  [products(): gathered = lax.all_gather(weighted, 'row', axis=0, tiled=True)]
  transfers between devices with their start and end apart: 3 -> 17, of which waited for: 3 -> 17; matrix products, arithmetic and copies ran while one was open for 0% -> 0% of each run, Pallas kernels for 0% -> 0%
where the time goes in v2:
time: 577 us; the launch traced here: 576 us
  blocking collectives  391 us (68%)
  waiting for transfers between devices  106 us (18%)
  matrix products  43.9 us (8%)
  other arithmetic  17 us (3%)
  between operations  13.2 us (2%)
    psum x2, blocking collectives, deflation(): lax.psum((jnp.sum(root_degree[:, None] * vectors, axis=0), jnp.sum(degree...  169 us
    psum x1, blocking collectives, local(): degree_set = lax.psum(row_sums, 'col')  121 us
    psum x1, blocking collectives, local(): lax.psum(jnp.dot(vectors.T, vectors, precision=lax.Precision.HIGHEST), ('...  77.3 us
    ppermute x14, waiting for transfers between devices, products(): now[kk] = jax.lax.ppermute(now[kk + 1], axis_name='row', perm=by_rank)  54.4 us
    all_gather x1, waiting for transfers between devices, local(): lax.all_gather(unit_rows, 'col', axis=0, tiled=True)  30.4 us
    unnamed x2, matrix products  26.3 us
    all_gather x1, blocking collectives, local(): column_set = lax.all_gather(unit_rows, 'row', axis=0, tiled=True)  24.6 us
    unnamed x5, waiting for transfers between devices  21.2 us
  transfers between devices with their start and end apart: 17, of which 17 were waited for; matrix products, arithmetic and copies ran while one was open for 0% of the time, Pallas kernels for 0%

profile of v2, /device:TPU:1, one launch (start us, length us, event | category | flops | bytes accessed | tf_op | source)
XLA Modules:
  0.0 576.4 jit_solution(11089118076547792525)
XLA Ops:
  6.5 1.0 fusion
  7.6 1.6 fusion.1
  9.2 24.6 %all_gather.7 = bf16[1536,256]{1,0:T(8,128)(2,1)S(1)} all-gather(bf16[192,256]{1,0:T(8,128)(2,1)} %fusion.1), channel_id=1, replica_groups=mesh['row'=8,'col'=32] {'row'}, dimensions={0}, use_global_device_ids=true | all-gather | bytes 884736 | tf_op jit(solution)/shard_map/all_gather | solution.py:18
  33.9 30.4 %all-gather.2.cloned.1.call-done = bf16[6144,256]{1,0:T(8,128)(2,1)} async-done(((bf16[192,256]{1,0:T(8,128)(2,1)}), bf16[6144,256]{1,0:T(8,128)(2,1)}) %all-gather.2.cloned.1.call-update) | async-done | bytes 3145744 | tf_op jit(solution)/shard_map/all_gather | solution.py:20
  64.2 16.3 %convert_reduce_fusion = (f32[6144]{0:T(1024)S(1)}, bf16[6144,1536]{0,1:T(8,128)(2,1)}) fusion(bf16[6144,256]{1,0:T(8,128)(2,1)} %all-gather.2.cloned.1.call-done, bf16[1536,256]{1,0:T(8,128)(2,1)S(1)} %all_gather.7), kind=kOutput, calls=%fused_computation | convolution fusion | flops 4907329536 | bytes 22831104 | tf_op jit(solution)/shard_map/dot_general | solution.py:19
  80.6 120.9 %psum.38 = f32[6144]{0:T(1024)S(1)} all-reduce(f32[6144]{0:T(1024)S(1)} %get-tuple-element.15), channel_id=1, replica_groups=mesh['row'=8,'col'=32] {'col'}, use_global_device_ids=true, to_apply=%region_2.0 | all-reduce | flops 6144 | bytes 49152 | tf_op jit(solution)/shard_map/psum | solution.py:27
  202.2 1.3 collective-permute-start
  203.6 3.1 collective-permute-done
  206.7 4.0 collective-permute-done.1
  210.7 4.0 collective-permute-done.2
  214.6 4.0 collective-permute-done.3
  218.6 4.5 collective-permute-done.4
  223.1 4.0 collective-permute-done.5
  227.1 4.0 collective-permute-done.6
  231.2 13.2 %fusion.6 = f32[6144,64]{1,0:T(8,128)} fusion(bf16[6144,1536]{0,1:T(8,128)(2,1)} %get-tuple-element.16, s32[]{:T(128)S(6)} %select_n.22, bf16[1536,64]{0,1:T(8,128)(2,1)S(1)} %concatenate.9), kind=kOutput, calls=%fused_computation.14 | convolution fusion | flops 1208352768 | bytes 20643844
  244.4 84.4 %all-reduce = (f32[64]{0:T(128)S(1)}, f32[]{:T(128)}) all-reduce(f32[64]{0:T(128)S(1)} %get-tuple-element.10, f32[]{:T(128)} %get-tuple-element.12), channel_id=1, replica_groups=mesh['row'=8,'col'=32] {'row','col'}, use_global_device_ids=true, to_apply=%region_5.7 | all-reduce | flops 65 | bytes 520 | tf_op jit(solution)/shard_map/psum | solution.py:55
  329.5 10.1 %reduce-scatter.7.cloned.1.call-done = f32[192,64]{1,0:T(8,128)} async-done(((f32[6144,64]{1,0:T(8,128)}), f32[192,64]{1,0:T(8,128)}) %reduce-scatter.7.cloned.1.call-update) | async-done | bytes 49168
  339.6 1.0 copy.9
  340.8 1.3 collective-permute-start.7
  342.1 3.1 collective-permute-done.7
  345.2 4.0 collective-permute-done.8
  349.2 4.0 collective-permute-done.9
  353.2 4.0 collective-permute-done.10
  357.1 4.0 collective-permute-done.11
  361.1 4.0 collective-permute-done.12
  365.1 4.0 collective-permute-done.13
  369.2 13.2 %fusion.3 = f32[6144,64]{1,0:T(8,128)} fusion(bf16[6144,1536]{0,1:T(8,128)(2,1)} %get-tuple-element.16, s32[]{:T(128)S(6)} %select_n.22, bf16[1536,64]{0,1:T(8,128)(2,1)S(1)} %concatenate.10), kind=kOutput, calls=%fused_computation.12 | convolution fusion | flops 1208352768 | bytes 20643844
  382.4 84.1 %psum.41 = f32[64]{0:T(128)S(1)} all-reduce(f32[64]{0:T(128)S(1)} %get-tuple-element.8), channel_id=1, replica_groups=mesh['row'=8,'col'=32] {'row','col'}, use_global_device_ids=true, to_apply=%region_10.12 | all-reduce | flops 64 | bytes 512 | tf_op jit(solution)/shard_map/psum | solution.py:55
  467.2 11.1 %reduce-scatter.9.cloned.1.call-done = f32[192,64]{1,0:T(8,128)} async-done(((f32[6144,64]{1,0:T(8,128)}), f32[192,64]{1,0:T(8,128)}) %reduce-scatter.9.cloned.1.call-update) | async-done | bytes 49168
  479.5 77.3 %psum.42 = f32[64,64]{0,1:T(8,128)S(1)} all-reduce(f32[64,64]{0,1:T(8,128)S(1)} %fusion.8), channel_id=1, replica_groups=mesh['row'=8,'col'=32] {'row','col'}, use_global_device_ids=true, to_apply=%region_11.13 | all-reduce | flops 4096 | bytes 32768 | tf_op jit(solution)/shard_map/psum | solution.py:74
  556.8 5.8 %cholesky.16 = f32[64,64]{1,0:T(8,128)S(1)} custom-call(f32[64,64]{1,0:T(8,128)S(1)} %fusion.11), custom_call_target="Cholesky" | custom-call | tf_op jit(solution)/shard_map/jit(cholesky)/cholesky | solution.py:77
  564.0 4.9 custom-call.6
  (36 shorter events, 6.3 us)
Async XLA Ops:
  6.5 57.7 %all-gather.2.cloned.1.call-start = ((), (), s32[]{:S(2)}) async-start(), calls=%async_computation.2 | async-start | bytes 3244032 | tf_op jit(solution)/shard_map/all_gather | solution.py:20
  9.2 330.5 %reduce-scatter.7.cloned.1.call-start = ((), (), s32[]{:S(2)}) async-start(), calls=%async_computation.3 | async-start | bytes 3244032
  33.9 168.2 %copy-start = (f32[192,64]{0,1:T(8,128)S(1)}, f32[192,64]{0,1:T(8,128)}, u32[]{:S(2)}) copy-start(f32[192,64]{0,1:T(8,128)} %param.5) | copy-start | bytes 147460
  202.2 4.5 collective-permute-start
  206.7 4.0 collective-permute-start.1
  210.7 4.0 collective-permute-start.2
  214.6 4.0 collective-permute-start.3
  218.6 4.5 collective-permute-start.4
  223.1 4.0 collective-permute-start.5
  227.1 4.0 collective-permute-start.6
  244.4 233.8 %reduce-scatter.9.cloned.1.call-start = ((), (), s32[]{:S(2)}) async-start(), calls=%async_computation.4 | async-start | bytes 3244032
  340.8 4.4 collective-permute-start.7
  345.2 4.0 collective-permute-start.8
  349.2 4.0 collective-permute-start.9
  353.2 4.0 collective-permute-start.10
  357.1 4.0 collective-permute-start.11
  361.1 4.0 collective-permute-start.12
  365.1 4.0 collective-permute-start.13
Sparse Core Ops, SparseCore 0:
  9.9 54.2 all-gather.1
  244.5 95.0 reduce-scatter.6
  382.5 95.6 reduce-scatter.8
